TPU v7x, 32 devices: a whole 2x2x4 slice. The times are simulated.
32 devices in a mesh: groups: 2 (over y), dp: 4 (over z), mx: 2 (over x), my: 2 (over core).
Axes of the slice: x: 2, y: 2, z: 4, core: 2. Of those that a mesh axis runs over, the one named last changes fastest.
Arguments:
- activations: bfloat16 [4096, 3072], P(('groups', 'dp', 'mx'), 'my'), parts along dimension 0, may hold values from -6 to 6
- ln_gain: float32 [3072], P('my'), may hold values from 0.5 to 1.5
- w_qkv: bfloat16 [3072, 24, 384], P('my', 'mx'), may hold values from -0.109375 to 0.109375
Outputs:
- context: bfloat16 [4096, 3072], P(('groups', 'dp', 'my'), 'mx'), parts along dimension 0
- h_input: float32 [6144, 3072], P(('groups', 'mx', 'my'), 'dp'), parts along dimension 0
- h_context: float32 [6144, 3072], P(('groups', 'mx'), ('dp', 'my')), parts along dimension 0
There are 2 independent parts, one for each index of `groups`. A program takes and returns all parts, laid end to end along the dimension named above; an argument that names none is the same for every part. Nothing has to cross between parts.
All inputs are finite; a program needn't handle non-finite values.
Results may differ from a plain program's by a relative error of at most 0.017.
Values may be sent and summed in bfloat16 or wider, within the bound.
A program may use at most 128 MiB of HBM per device.

v0:
```python
import jax
import jax.numpy as jnp
from jax import lax
from jax.sharding import PartitionSpec as P

EPSILON = 1e-06


def spread_2(block, axis, owner):
    block = jnp.where(lax.axis_index(axis) == owner, block, jnp.zeros_like(block))
    return lax.psum(block, axis)


def layer_norm(inputs):
    average = jnp.mean(inputs, -1, keepdims=True)
    squares = jnp.mean(inputs * inputs, -1, keepdims=True)
    return (inputs - average) * lax.rsqrt(squares - average * average + EPSILON)


def gram_product(left_side, right_side):
    return lax.dot_general(
        left_side, right_side, (((0,), (0,)), ((), ())), preferred_element_type=jnp.float32
    )


def on_device(activations, ln_gain, w_qkv):
    row_count, feature_count = activations.shape
    widened = activations.astype(jnp.float32)
    row_sums, row_squares = lax.psum((jnp.sum(widened, 1), jnp.sum(widened * widened, 1)), "my")
    width = feature_count * lax.axis_size("my")
    average = (row_sums / width)[:, None]
    spread = (row_squares / width)[:, None] - average * average
    normed = ((widened - average) * lax.rsqrt(spread + EPSILON) * ln_gain).astype(jnp.bfloat16)
    image_rows = lax.all_gather(normed, "mx", axis=0, tiled=True)
    local_heads, triple = (w_qkv.shape[1], w_qkv.shape[2])
    head_size = triple // 3
    flat_weight = w_qkv.reshape(feature_count, local_heads * triple)
    own_rows = image_rows.shape[0] // lax.axis_size("my")
    projected = (
        lax.psum_scatter(
            jnp.dot(image_rows, flat_weight, preferred_element_type=jnp.float32).astype(
                jnp.bfloat16
            ),
            "my",
            scatter_dimension=0,
            tiled=True,
        )
        .astype(jnp.float32)
        .reshape(own_rows, local_heads, triple)
    )
    queries = layer_norm(projected[:, :, :head_size]).astype(jnp.bfloat16)
    key_rows = layer_norm(projected[:, :, head_size : 2 * head_size]).astype(jnp.bfloat16)
    value_rows = projected[:, :, 2 * head_size :].astype(jnp.bfloat16)
    all_keys, all_values = (
        lax.all_gather(key_rows, "my", axis=0, tiled=True),
        lax.all_gather(value_rows, "my", axis=0, tiled=True),
    )
    scores = jnp.einsum(
        "qhd,khd->hqk", queries, all_keys, preferred_element_type=jnp.float32
    ) * head_size ** (-0.5)
    powers = jnp.exp(scores)
    totals = jnp.sum(powers, 2)
    weights = powers.astype(jnp.bfloat16)
    mixture = jnp.einsum("hqk,khd->qhd", weights, all_values, preferred_element_type=jnp.float32)
    mixture = mixture / jnp.transpose(totals)[:, :, None]
    context = mixture.astype(jnp.bfloat16).reshape(own_rows, local_heads * head_size)
    full_rows = lax.all_gather(image_rows, "my", axis=1, tiled=True)
    tile_width = full_rows.shape[1] // (lax.axis_size("mx") * lax.axis_size("my"))
    tile_index = lax.axis_index("mx") * lax.axis_size("my") + lax.axis_index("my")
    row_block = lax.dynamic_slice_in_dim(full_rows, tile_index * tile_width, tile_width, 1)
    factor = 2.0 / (full_rows.shape[0] * lax.axis_size("dp"))
    h_input = (
        lax.psum_scatter(
            gram_product(row_block, full_rows).astype(jnp.bfloat16),
            "dp",
            scatter_dimension=1,
            tiled=True,
        ).astype(jnp.float32)
        * factor
    )
    everything = lax.all_gather(context, ("dp", "my"), axis=0, tiled=True)
    block_width = everything.shape[1]
    narrow = block_width * lax.axis_size("mx") // (lax.axis_size("dp") * lax.axis_size("my"))
    flat_index = lax.axis_index("dp") * lax.axis_size("my") + lax.axis_index("my")
    offset = flat_index * narrow
    column_piece = lax.dynamic_slice_in_dim(everything, offset % block_width, narrow, 1)
    columns = spread_2(column_piece, "mx", offset // block_width)
    h_context = gram_product(everything, columns) * factor
    return (context, h_input, h_context)


def solution(mesh):
    placed = (P(("groups", "dp", "mx"), "my"), P("my"), P("my", "mx", None))
    return jax.shard_map(
        on_device,
        mesh=mesh,
        in_specs=placed,
        out_specs=(
            P(("groups", "dp", "my"), "mx"),
            P(("groups", "mx", "my"), "dp"),
            P(("groups", "mx"), ("dp", "my")),
        ),
        check_vma=False,
    )
```

profile of v0, /device:TPU:7, one launch (start us, length us, event | category | flops | bytes accessed | tf_op | source)
XLA Modules:
  0.0 341.0 jit_solution(9555886501262374267)
XLA Ops:
  7.2 1.5 convert_reduce_fusion
  8.7 2.8 all-reduce
  11.5 2.3 fusion.7
  13.9 0.0 reduce-scatter.3.cloned.1.call-start
  13.9 18.7 %copy.9 = bf16[1536,12,384]{0,2,1:T(8,128)(2,1)} copy(bf16[1536,12,384]{2,0,1:T(8,128)(2,1)} %param.5) | data formatting | bytes 28311552 | tf_op args[2]
  32.7 8.5 %all-gather.6.cloned.1.call-done = bf16[512,1536]{1,0:T(8,128)(2,1)} async-done(((bf16[256,1536]{1,0:T(8,128)(2,1)}), bf16[512,1536]{1,0:T(8,128)(2,1)}) %all-gather.6.cloned.1.call-update) | async-done | bytes 1572880 | tf_op jit(solution)/shard_map/all_gather | solution.py:34
  41.2 12.6 %convolution_convert_fusion = bf16[512,4608]{1,0:T(8,128)(2,1)} fusion(bf16[512,1536]{1,0:T(8,128)(2,1)} %all-gather.6.cloned.1.call-done, bf16[1536,4608]{0,1:T(8,128)(2,1)} %bitcast.15), kind=kOutput, calls=%fused_computation | convolution fusion | flops 7250116608 | bytes 20447232 | tf_op jit(solution)/shard_map/dot_general | solution.py:41
  53.8 0.0 all-gather.10.cloned.1.call-start
  53.9 14.4 %reduce-scatter.3.cloned.1.call-done = bf16[256,4608]{1,0:T(8,128)(2,1)} async-done(((bf16[512,4608]{1,0:T(8,128)(2,1)}), bf16[256,4608]{1,0:T(8,128)(2,1)}) %reduce-scatter.3.cloned.1.call-update) | async-done | bytes 2359312 | tf_op jit(solution)/shard_map/reduce_scatter | solution.py:40
  68.2 2.8 copy.10
  71.1 2.4 copy.11
  73.5 2.1 reshape.64
  75.6 1.7 slice_reduce_fusion.1
  77.3 0.5 copy-done
  77.8 1.7 multiply_convert_fusion
  79.6 0.0 all-gather.8.cloned.1.call-start
  79.6 0.9 slice.13
  80.6 0.5 all-gather.12.cloned.1.call-update
  81.2 9.5 %all-gather.10.cloned.1.call-done = bf16[512,12,128]{2,0,1:T(8,128)(2,1)} async-done(((bf16[256,12,128]{2,0,1:T(8,128)(2,1)}), bf16[512,12,128]{2,0,1:T(8,128)(2,1)}) %all-gather.10.cloned.1.call-update) | async-done | bytes 1572880 | tf_op jit(solution)/shard_map/all_gather | solution.py:55
  90.7 5.9 %fusion = (f32[12,256]{1,0:T(8,128)S(1)}, f32[12,256,512]{2,1,0:T(8,128)}) fusion(bf16[512,12,128]{2,0,1:T(8,128)(2,1)} %all-gather.10.cloned.1.call-done, f32[256,12,384]{2,0,1:T(8,128)} %copy-done, f32[256,12]{0,1:T(8,128)S(1)} %get-tuple-element.18, f32[256,12]{0,1:T(8,128)S(1)} %get-tuple-element.17), kind=kOutput, calls=%fused_computation.2 | convolution fusion | flops 406975488 | bytes 9474048 | tf_op jit(solution)/shard_map/qhd,khd->hqk/dot_general | solution.py:58
  96.5 7.0 %all-gather.8.cloned.1.call-done = bf16[512,12,128]{0,2,1:T(8,128)(2,1)} async-done(((bf16[256,12,128]{0,2,1:T(8,128)(2,1)}), bf16[512,12,128]{0,2,1:T(8,128)(2,1)}) %all-gather.8.cloned.1.call-update) | async-done | bytes 1572880 | tf_op jit(solution)/shard_map/all_gather | solution.py:56
  103.6 5.3 %fusion.9 = bf16[256,12,128]{0,2,1:T(8,128)(2,1)} fusion(bf16[512,12,128]{0,2,1:T(8,128)(2,1)} %all-gather.8.cloned.1.call-done, f32[12,256,512]{2,1,0:T(8,128)} %get-tuple-element.24, f32[256,12]{0,1:T(8,128)S(1)} %bitcast.20), kind=kOutput, calls=%fused_computation.17 | convolution fusion | flops 406585344 | bytes 8663040 | tf_op jit(solution)/shard_map/hqk,khd->qhd/dot_general | solution.py:64
  109.0 9.4 %all-gather.12.cloned.1.call-done = bf16[512,3072]{1,0:T(8,128)(2,1)} async-done(((bf16[512,1536]{1,0:T(8,128)(2,1)}), bf16[512,3072]{1,0:T(8,128)(2,1)}) %all-gather.12.cloned.1.call-update) | async-done | bytes 3145744 | tf_op jit(solution)/shard_map/all_gather | solution.py:67
  118.4 7.0 %convolution_convert_fusion.1 = bf16[768,3072]{1,0:T(8,128)(2,1)} fusion(bf16[512,3072]{1,0:T(8,128)(2,1)} %all-gather.12.cloned.1.call-done, s32[]{:T(128)S(6)} %select_n.25), kind=kOutput, calls=%fused_computation.4 | convolution fusion | flops 2418278400 | bytes 8650756 | tf_op jit(solution)/shard_map/dot_general | solution.py:21
  125.4 0.2 all-reduce.3.cloned.1.call-start
  125.7 60.9 %all-gather.14.cloned.1.call-done = bf16[2048,1536]{0,1:T(8,128)(2,1)} async-done(((bf16[256,1536]{0,1:T(8,128)(2,1)}), bf16[2048,1536]{0,1:T(8,128)(2,1)}) %all-gather.14.cloned.1.call-update) | async-done | bytes 6291472 | tf_op jit(solution)/shard_map/all_gather | solution.py:81
  186.6 3.1 dynamic-slice_select_fusion
  189.7 1.2 copy.12
  190.8 81.3 %reduce-scatter.5.cloned.1.call-done = bf16[768,768]{1,0:T(8,128)(2,1)} async-done(((bf16[768,3072]{1,0:T(8,128)(2,1)}), bf16[768,768]{1,0:T(8,128)(2,1)}) %reduce-scatter.5.cloned.1.call-update) | async-done | bytes 1179664 | tf_op jit(solution)/shard_map/reduce_scatter | solution.py:73
  272.1 2.8 convert_multiply_fusion.1
  274.9 51.2 %all-reduce.3.cloned.1.call-done = bf16[2048,384]{0,1:T(8,128)(2,1)} async-done(((bf16[2048,384]{0,1:T(8,128)(2,1)}), bf16[2048,384]{0,1:T(8,128)(2,1)}) %all-reduce.3.cloned.1.call-update) | async-done | bytes 1572880 | tf_op jit(solution)/shard_map/psum | solution.py:11
  326.1 8.1 %convolution_multiply_fusion = f32[1536,384]{1,0:T(8,128)} fusion(bf16[2048,1536]{0,1:T(8,128)(2,1)} %all-gather.14.cloned.1.call-done, bf16[2048,384]{0,1:T(8,128)(2,1)} %all-reduce.3.cloned.1.call-done), kind=kOutput, calls=%fused_computation.7 | convolution fusion | flops 2416508928 | bytes 10223616 | tf_op jit(solution)/shard_map/dot_general | solution.py:21
  (17 shorter events, 0.3 us)
Async XLA Ops:
  7.2 34.0 %all-gather.6.cloned.1.call-start = ((), (), s32[]{:S(2)}) async-start(), calls=%async_computation.2 | async-start | bytes 2359296 | tf_op jit(solution)/shard_map/all_gather | solution.py:34
  13.9 54.4 %reduce-scatter.3.cloned.1.call-start = ((), (), s32[]{:S(2)}) async-start(), calls=%async_computation.3 | async-start | bytes 7077888 | tf_op jit(solution)/shard_map/reduce_scatter | solution.py:40
  53.8 36.9 %all-gather.10.cloned.1.call-start = ((), (), s32[]{:S(2)}) async-start(), calls=%async_computation.5 | async-start | bytes 2359296 | tf_op jit(solution)/shard_map/all_gather | solution.py:55
  75.6 2.2 copy-start
  79.6 24.0 %all-gather.8.cloned.1.call-start = ((), (), s32[]{:S(2)}) async-start(), calls=%async_computation.4 | async-start | bytes 2359296 | tf_op jit(solution)/shard_map/all_gather | solution.py:56
  80.6 37.8 %all-gather.12.cloned.1.call-start = ((), (), s32[]{:S(2)}) async-start(), calls=%async_computation.6 | async-start | bytes 4718592 | tf_op jit(solution)/shard_map/all_gather | solution.py:67
  81.2 105.4 %all-gather.14.cloned.1.call-start = ((), (), s32[]{:S(2)}) async-start(), calls=%async_computation.8 | async-start | bytes 7077888 | tf_op jit(solution)/shard_map/all_gather | solution.py:81
  108.9 163.2 %reduce-scatter.5.cloned.1.call-start = ((), (), s32[]{:S(2)}) async-start(), calls=%async_computation.7 | async-start | bytes 5898240 | tf_op jit(solution)/shard_map/reduce_scatter | solution.py:73
  125.4 200.7 %all-reduce.3.cloned.1.call-start = ((), (), s32[]{:S(2)}) async-start(), calls=%async_computation.9 | async-start | bytes 3145728 | tf_op jit(solution)/shard_map/psum | solution.py:11
  125.7 64.0 %copy-start.1 = (bf16[256,12,128]{0,2,1:T(8,128)(2,1)S(1)}, bf16[256,12,128]{0,2,1:T(8,128)(2,1)}, u32[]{:S(2)}) copy-start(bf16[256,12,128]{0,2,1:T(8,128)(2,1)} %fusion.9) | copy-start | bytes 2359300
Sparse Core Ops, SparseCore 0:
  14.0 27.1 all-gather.5
  53.9 14.2 reduce-scatter.2
  79.7 10.9 all-gather.9
  92.7 10.8 all-gather.7
  105.0 13.3 all-gather.11
  120.5 66.0 all-gather.13
  189.0 83.0 reduce-scatter.4
  275.1 51.0 all-reduce.2
where the time goes:
time: 344 us; the launch traced here: 341 us
  waiting for transfers between devices  243 us (71%)
  matrix products  38.9 us (11%)
  local copies, waits for them, and re-layouts  26.6 us (8%)
  other arithmetic  15.2 us (4%)
  between operations  14.3 us (4%)
    reduce_scatter x1, waiting for transfers between devices, on_device(): lax.psum_scatter(gram_product(row_block, full_rows).astype(jnp.bfloat16),...  81.3 us
    all_gather x1, waiting for transfers between devices, on_device(): everything = lax.all_gather(context, ('dp', 'my'), axis=0, tiled=True)  60.9 us
    psum x1, waiting for transfers between devices, spread_2(): return lax.psum(block, axis)  51.2 us
    unnamed x6, local copies, waits for them, and re-layouts  20.4 us
    dot_general x2, matrix products, gram_product(): lax.dot_general(left_side, right_side, (((0,), (0,)), ((), ())), preferre...  15.1 us
    reduce_scatter x1, waiting for transfers between devices, on_device(): lax.psum_scatter(jnp.dot(image_rows, flat_weight, preferred_element_type=...  14.4 us
    dot_general x1, matrix products, on_device(): jnp.dot(image_rows, flat_weight, preferred_element_type=jnp.float32)  12.6 us
    all_gather x1, waiting for transfers between devices, on_device(): lax.all_gather(key_rows, 'my', axis=0, tiled=True)  9.47 us
  transfers between devices with their start and end apart: 8, of which 8 were waited for; matrix products, arithmetic and copies ran while one was open for 13% of the time, Pallas kernels for 0%

commit v1 on v0

--- a/solution.py
+++ b/solution.py
@@ -1,9 +1,14 @@
+import functools
+
 import jax
 import jax.numpy as jnp
 from jax import lax
+from jax.experimental import pallas as pl
+from jax.experimental.pallas import tpu as pltpu
 from jax.sharding import PartitionSpec as P
 
 EPSILON = 1e-06
+MESH = pl.DeviceIdType.MESH
 
 
 def spread_2(block, axis, owner):
@@ -89,10 +94,415 @@
     return (context, h_input, h_context)
 
 
+class Gather:
+    def __init__(self, length, place, rows, columns, total, send, receive, share, shared, local):
+        self.length, (self.z, self.x, self.c) = length, place
+        self.rows, self.columns, self.total = rows, columns, total
+        self.send, self.receive = send, receive
+        self.share, self.shared, self.local = share, shared, local
+        block = 2 * self.x + self.c
+        self.owner = block == self.z
+        self.relay = (self.x != self.z // 2) & (self.c == self.z % 2)
+
+    def image(self, way, step):
+        return self.z - step if way == 0 else self.z + step
+
+    def valid(self, way, step):
+        return self.z >= step if way == 0 else self.z + step < self.length
+
+    def hop(self, way, step):
+        image = self.image(way, step)
+        return pltpu.make_async_remote_copy(
+            src_ref=self.rows.at[image],
+            dst_ref=self.rows.at[image],
+            send_sem=self.send.at[way, step],
+            recv_sem=self.receive.at[way, step],
+            device_id={"dp": self.z + 1 if way == 0 else self.z - 1},
+            device_id_type=MESH,
+        )
+
+    def hops(self, way, step):
+        inside = self.z < self.length - 1 if way == 0 else self.z > 0
+        return inside & self.valid(way, step)
+
+    def arrival(self, way, step):
+        image = self.image(way, step)
+        return pltpu.make_async_remote_copy(
+            src_ref=self.rows.at[image],
+            dst_ref=self.rows.at[image],
+            send_sem=self.send.at[way, step],
+            recv_sem=self.receive.at[way, step - 1],
+            device_id={"dp": self.z - 1 if way == 0 else self.z + 1},
+            device_id_type=MESH,
+        )
+
+    def sharing(self, source, image, axis):
+        other = {"my": 1 - self.c} if axis == 0 else {"mx": 1 - self.x}
+        return pltpu.make_async_remote_copy(
+            src_ref=source.at[image],
+            dst_ref=self.columns.at[image],
+            send_sem=self.share.at[image, axis],
+            recv_sem=self.shared.at[image],
+            device_id=other,
+            device_id_type=MESH,
+        )
+
+    def own(self, image):
+        return pltpu.make_async_copy(
+            self.rows.at[image], self.columns.at[image], self.local.at[image]
+        )
+
+    def spread(self, image):
+        @pl.when(self.owner)
+        def _():
+            self.sharing(self.rows, image, 1).start()
+            self.sharing(self.rows, image, 0).start()
+            self.own(image).start()
+
+    def begin(self):
+        for way in range(2):
+
+            @pl.when(self.hops(way, 0))
+            def _():
+                self.hop(way, 0).start()
+
+        self.spread(self.z)
+
+    def forward(self, step):
+        for way in range(2):
+
+            @pl.when(self.valid(way, step))
+            def _():
+                self.arrival(way, step).wait_recv()
+                if step < self.length - 1:
+
+                    @pl.when(self.hops(way, step))
+                    def _():
+                        self.hop(way, step).start()
+
+                self.spread(self.image(way, step))
+
+    def take(self, image, first):
+        @pl.when(self.owner)
+        def _():
+            self.own(image).wait()
+
+        @pl.when(jnp.logical_not(self.owner))
+        def _():
+            self.sharing(self.rows, image, 0).wait_recv()
+
+        @pl.when(self.relay)
+        def _():
+            self.sharing(self.columns, image, 0).start()
+
+        def piece(index, carry):
+            part = pl.ds(pl.multiple_of(index * 256, 256), 256)
+            term = lax.dot_general(
+                self.rows[image, :, part],
+                self.columns[image],
+                (((0,), (0,)), ((), ())),
+                preferred_element_type=jnp.float32,
+            )
+            if first:
+                self.total[part, :] = term
+            else:
+                self.total[part, :] += term
+            return carry
+
+        lax.fori_loop(0, self.total.shape[0] // 256, piece, 0)
+
+    def consume(self, step):
+        if step == 0:
+            self.take(self.z, True)
+            return
+        for way in range(2):
+
+            @pl.when(self.valid(way, step))
+            def _():
+                self.take(self.image(way, step), False)
+
+    def finish(self):
+        for way in range(2):
+            for step in range(self.length - 1):
+
+                @pl.when(self.hops(way, step))
+                def _():
+                    self.hop(way, step).wait_send()
+
+        def one(image, carry):
+            @pl.when(self.owner)
+            def _():
+                self.sharing(self.rows, image, 1).wait_send()
+                self.sharing(self.rows, image, 0).wait_send()
+
+            @pl.when(self.relay)
+            def _():
+                self.sharing(self.columns, image, 0).wait_send()
+
+            return carry
+
+        lax.fori_loop(0, self.length, one, 0)
+
+
+def kernel(
+    length, factor, head_size,
+    image_ref, weight_ref, context_ref, input_ref, gram_ref,
+    weights, leaving, kept, arrived,
+    input_rows, input_columns, context_rows, context_columns, total,
+    weight_sem, plane_sem, part_send, part_receive,
+    line_send, line_receive, share_send, share_receive, local_sem, swap_sem,
+):
+    z, x, c = lax.axis_index("dp"), lax.axis_index("mx"), lax.axis_index("my")
+    heads, _, triple = weights.shape
+    half = heads // 2
+    tokens, block = input_rows.shape[1:]
+
+    def weight_copy(position):
+        head = lax.rem(position + (1 - c) * half, heads)
+        columns = pl.ds(pl.multiple_of(head * triple, triple), triple)
+        return pltpu.make_async_copy(
+            weight_ref.at[:, columns], weights.at[position], weight_sem.at[position]
+        )
+
+    def start_weight(position, carry):
+        weight_copy(position).start()
+        return carry
+
+    lax.fori_loop(0, heads, start_weight, 0)
+
+    barrier = pltpu.get_barrier_semaphore()
+    pl.semaphore_signal(barrier, inc=1, device_id={"my": 1 - c}, device_id_type=MESH)
+    pl.semaphore_signal(barrier, inc=1, device_id={"mx": 1 - x}, device_id_type=MESH)
+
+    @pl.when(z > 0)
+    def _():
+        pl.semaphore_signal(barrier, inc=1, device_id={"dp": z - 1}, device_id_type=MESH)
+
+    @pl.when(z < length - 1)
+    def _():
+        pl.semaphore_signal(barrier, inc=1, device_id={"dp": z + 1}, device_id_type=MESH)
+
+    edges = jnp.where(z > 0, 1, 0) + jnp.where(z < length - 1, 1, 0)
+    pl.semaphore_wait(barrier, 2 + edges)
+
+    inputs = Gather(
+        length, (z, x, c), input_rows, input_columns, input_ref,
+        line_send.at[0], line_receive.at[0], share_send.at[0], share_receive.at[0], local_sem.at[0],
+    )
+    contexts = Gather(
+        length, (z, x, c), context_rows, context_columns, total,
+        line_send.at[1], line_receive.at[1], share_send.at[1], share_receive.at[1], local_sem.at[1],
+    )
+
+    def plane_copy():
+        return pltpu.make_async_remote_copy(
+            src_ref=image_ref.at[:, pl.ds(pl.multiple_of((1 - c) * block, block), block)],
+            dst_ref=input_rows.at[z],
+            send_sem=plane_sem.at[0],
+            recv_sem=plane_sem.at[1],
+            device_id={"my": 1 - c},
+            device_id_type=MESH,
+        )
+
+    @pl.when(c == x)
+    def _():
+        plane_copy().start()
+        mine = pl.ds(pl.multiple_of(c * block, block), block)
+        keep = pltpu.make_async_copy(image_ref.at[:, mine], input_rows.at[z], plane_sem.at[2])
+        keep.start()
+        keep.wait()
+
+    @pl.when(c != x)
+    def _():
+        plane_copy().wait_recv()
+
+    inputs.begin()
+
+    def part_copy(index):
+        return pltpu.make_async_remote_copy(
+            src_ref=leaving.at[index],
+            dst_ref=arrived.at[index],
+            send_sem=part_send.at[index],
+            recv_sem=part_receive.at[index],
+            device_id={"my": 1 - c},
+            device_id_type=MESH,
+        )
+
+    def project_away(index, carry):
+        weight_copy(index).wait()
+        leaving[index] = jnp.dot(
+            image_ref[...], weights[index], preferred_element_type=jnp.float32
+        ).astype(jnp.bfloat16)
+        part_copy(index).start()
+        return carry
+
+    lax.fori_loop(0, half, project_away, 0)
+
+    def project_here(index, carry):
+        weight_copy(half + index).wait()
+        kept[index] = jnp.dot(
+            image_ref[...], weights[half + index], preferred_element_type=jnp.float32
+        ).astype(jnp.bfloat16)
+        return carry
+
+    lax.fori_loop(0, half, project_here, 0)
+
+    inputs.forward(1)
+
+    def norm(values):
+        average = jnp.mean(values, -1, keepdims=True)
+        squares = jnp.mean(values * values, -1, keepdims=True)
+        return ((values - average) * lax.rsqrt(squares - average * average + EPSILON)).astype(
+            jnp.bfloat16
+        )
+
+    def attend(index, carry):
+        part_copy(index).wait_recv()
+        projected = kept[index].astype(jnp.float32) + arrived[index].astype(jnp.float32)
+        queries = norm(projected[:, :head_size])
+        keys = norm(projected[:, head_size : 2 * head_size])
+        values = projected[:, 2 * head_size :].astype(jnp.bfloat16)
+        scores = lax.dot_general(
+            queries, keys, (((1,), (1,)), ((), ())), preferred_element_type=jnp.float32
+        ) * head_size ** (-0.5)
+        powers = jnp.exp(scores)
+        totals = jnp.sum(powers, 1, keepdims=True)
+        mixture = jnp.dot(
+            powers.astype(jnp.bfloat16), values, preferred_element_type=jnp.float32
+        )
+        place = pl.ds(pl.multiple_of(index * head_size, head_size), head_size)
+        context_rows[z, :, place] = (mixture / totals).astype(jnp.bfloat16)
+        return carry
+
+    lax.fori_loop(0, half, attend, 0)
+    contexts.begin()
+
+    own_tokens = tokens // 2
+    place = pl.ds(pl.multiple_of(c * block, block), block)
+
+    def context_copy():
+        away = pl.ds(pl.multiple_of((1 - c) * own_tokens, own_tokens), own_tokens)
+        return pltpu.make_async_remote_copy(
+            src_ref=context_rows.at[z, away],
+            dst_ref=context_ref.at[:, place],
+            send_sem=swap_sem.at[0],
+            recv_sem=swap_sem.at[1],
+            device_id={"my": 1 - c},
+            device_id_type=MESH,
+        )
+
+    context_copy().start()
+    here = pl.ds(pl.multiple_of(c * own_tokens, own_tokens), own_tokens)
+    context_keep = pltpu.make_async_copy(
+        context_rows.at[z, here], context_ref.at[:, place], swap_sem.at[2]
+    )
+    context_keep.start()
+
+    inputs.consume(0)
+    inputs.forward(2)
+    inputs.consume(1)
+    contexts.forward(1)
+    contexts.consume(0)
+    for step in range(3, length):
+        inputs.forward(step)
+        inputs.consume(step - 1)
+        contexts.forward(step - 1)
+        contexts.consume(step - 2)
+    inputs.consume(length - 1)
+    input_ref[...] = input_ref[...] * factor
+    contexts.forward(length - 1)
+    contexts.consume(length - 2)
+    contexts.consume(length - 1)
+
+    narrow = block // 2
+    rows = pl.ds(pl.multiple_of(c * block, block), block)
+    total[...] = total[...] * factor
+
+    def gram_copy():
+        return pltpu.make_async_remote_copy(
+            src_ref=total.at[:, pl.ds(pl.multiple_of((1 - c) * narrow, narrow), narrow)],
+            dst_ref=gram_ref.at[rows],
+            send_sem=swap_sem.at[3],
+            recv_sem=swap_sem.at[4],
+            device_id={"my": 1 - c},
+            device_id_type=MESH,
+        )
+
+    gram_copy().start()
+    gram_ref[rows, :] = total[:, pl.ds(pl.multiple_of(c * narrow, narrow), narrow)]
+
+    @pl.when(c == x)
+    def _():
+        plane_copy().wait_send()
+
+    def part_sent(index, carry):
+        part_copy(index).wait_send()
+        return carry
+
+    lax.fori_loop(0, half, part_sent, 0)
+    inputs.finish()
+    contexts.finish()
+    context_keep.wait()
+    context_copy().wait()
+    gram_copy().wait()
+
+
+def on_device_fused(activations, ln_gain, w_qkv):
+    row_count, feature_count = activations.shape
+    widened = activations.astype(jnp.float32)
+    row_sums, row_squares = lax.psum((jnp.sum(widened, 1), jnp.sum(widened * widened, 1)), "my")
+    width = feature_count * lax.axis_size("my")
+    average = (row_sums / width)[:, None]
+    spread = (row_squares / width)[:, None] - average * average
+    normed = ((widened - average) * lax.rsqrt(spread + EPSILON) * ln_gain).astype(jnp.bfloat16)
+    image_rows = lax.all_gather(normed, "mx", axis=0, tiled=True)
+    heads, triple = w_qkv.shape[1:]
+    flat_weight = w_qkv.reshape(feature_count, heads * triple)
+    length, tokens, block = lax.axis_size("dp"), image_rows.shape[0], feature_count // 2
+    gathered = pltpu.VMEM((length, tokens, block), jnp.bfloat16)
+    part = pltpu.VMEM((heads // 2, tokens, triple), jnp.bfloat16)
+    dma = pltpu.SemaphoreType.DMA
+    whole = pl.BlockSpec(memory_space=pltpu.VMEM)
+    return pl.pallas_call(
+        functools.partial(kernel, length, 2.0 / (tokens * length), triple // 3),
+        out_shape=(
+            jax.ShapeDtypeStruct((tokens // 2, 2 * block), jnp.bfloat16),
+            jax.ShapeDtypeStruct((block, block), jnp.float32),
+            jax.ShapeDtypeStruct((2 * block, block // 2), jnp.float32),
+        ),
+        in_specs=[whole, pl.BlockSpec(memory_space=pl.ANY)],
+        out_specs=(whole, whole, whole),
+        scratch_shapes=[
+            pltpu.VMEM((heads, feature_count, triple), jnp.bfloat16),
+            part, part, part,
+            gathered, gathered, gathered, gathered,
+            pltpu.VMEM((block, block), jnp.float32),
+            dma((heads,)),
+            dma((3,)),
+            dma((heads // 2,)),
+            dma((heads // 2,)),
+            dma((2, 2, length)),
+            dma((2, 2, length)),
+            dma((2, length, 2)),
+            dma((2, length)),
+            dma((2, length)),
+            dma((5,)),
+        ],
+        compiler_params=pltpu.CompilerParams(
+            collective_id=0, has_side_effects=True, vmem_limit_bytes=60 * 1024 * 1024
+        ),
+        cost_estimate=pl.CostEstimate(
+            flops=14_000_000_000, bytes_accessed=24_000_000, transcendentals=2_000_000
+        ),
+        name="attention_grams",
+    )(image_rows, flat_weight)
+
+
 def solution(mesh):
     placed = (P(("groups", "dp", "mx"), "my"), P("my"), P("my", "mx", None))
+    fused = mesh.shape["mx"] == 2 and mesh.shape["my"] == 2 and mesh.shape["dp"] == 4
     return jax.shard_map(
-        on_device,
+        on_device_fused if fused else on_device,
         mesh=mesh,
         in_specs=placed,
         out_specs=(

time: 344 us -> 194 us (0.56)
  waiting for transfers between devices: 243 us -> 0.02 us
  Pallas kernels: 0 us -> 128 us
  matrix products: 38.9 us -> 0 us
  local copies, waits for them, and re-layouts: 26.6 us -> 44.4 us
  other arithmetic: 15.2 us -> 3.82 us
    pallas_call x0 -> x1, Pallas kernels: none -> 128 us  [on_device_fused(): pl.pallas_call(functools.partial(kernel, length, 2.0 / (tokens * length),...]
    reduce_scatter x2 -> x0, waiting for transfers between devices: 95.6 us -> none  [the longest x1 81.3 us: on_device(): lax.psum_scatter(gram_product(row_block, full_rows).astype(jnp.bfloat16),...]
    all_gather x5 -> x1, waiting for transfers between devices: 95.3 us -> 0.01 us  [on_device_fused(): image_rows = lax.all_gather(normed, 'mx', axis=0, tiled=True)]
    psum x1 -> x0, waiting for transfers between devices: 51.2 us -> none  [spread_2(): return lax.psum(block, axis)]
    dot_general x5 -> x0, matrix products: 38.9 us -> none  [the longest x2 15.1 us: gram_product(): lax.dot_general(left_side, right_side, (((0,), (0,)), ((), ())), preferre...]
    reshape x1, local copies, waits for them, and re-layouts: 2.43 us -> 18.8 us  [on_device_fused(): flat_weight = w_qkv.reshape(feature_count, heads * triple)]
    unnamed x6, local copies, waits for them, and re-layouts: 20.4 us -> 25.6 us
  transfers between devices with their start and end apart: 8 -> 1, of which waited for: 8 -> 0; matrix products, arithmetic and copies ran while one was open for 13% -> 19% of each run, Pallas kernels for 0% -> 0%
where the time goes in v1:
time: 194 us; the launch traced here: 193 us
  Pallas kernels  128 us (66%)
  local copies, waits for them, and re-layouts  44.4 us (23%)
  between operations  14 us (7%)
  other arithmetic  3.82 us (2%)
  blocking collectives  2.8 us (1%)
    pallas_call x1, Pallas kernels, on_device_fused(): pl.pallas_call(functools.partial(kernel, length, 2.0 / (tokens * length),...  128 us
    unnamed x6, local copies, waits for them, and re-layouts  25.6 us
    reshape x1, local copies, waits for them, and re-layouts, on_device_fused(): flat_weight = w_qkv.reshape(feature_count, heads * triple)  18.8 us
  transfers between devices with their start and end apart: 1, of which 0 were waited for; matrix products, arithmetic and copies ran while one was open for 19% of the time, Pallas kernels for 0%

profile of v1, /device:TPU:7, one launch (start us, length us, event | category | flops | bytes accessed | tf_op | source)
XLA Modules:
  0.0 192.9 jit_solution(635069170004241172)
XLA Ops:
  7.2 0.0 all-gather.2.cloned.1.call-start
  7.2 1.5 convert_reduce_fusion
  8.7 2.8 %all-reduce = (f32[256]{0:T(256)S(1)}, f32[256]{0:T(256)S(1)}) all-reduce(f32[256]{0:T(256)S(1)} %get-tuple-element.4, f32[256]{0:T(256)S(1)} %get-tuple-element.3), channel_id=1, replica_groups=mesh['groups'=2,'dp'=4,'mx'=2,'my'=2] {'my'}, use_global_device_ids=true, to_apply=%region_3.0 | all-reduce | flops 512 | bytes 4096 | tf_op jit(solution)/shard_map/psum | solution.py:453
  11.5 2.3 %fusion.2 = bf16[256,1536]{1,0:T(8,128)(2,1)} fusion(bf16[256,1536]{1,0:T(8,128)(2,1)} %param.3, f32[1536]{0:T(1024)} %param.4, f32[256]{0:T(256)S(1)} %get-tuple-element.8, f32[256]{0:T(256)S(1)} %get-tuple-element.7), kind=kLoop, calls=%fused_computation.5 | loop fusion | flops 1966080 | bytes 1581056 | tf_op jit(solution)/shard_map/convert_element_type | solution.py:457
  13.8 0.0 all-gather.2.cloned.1.call-update
  13.9 18.7 %copy.7 = bf16[1536,12,384]{0,2,1:T(8,128)(2,1)} copy(bf16[1536,12,384]{2,0,1:T(8,128)(2,1)} %param.5) | data formatting | bytes 28311552 | tf_op args[2]
  32.6 18.8 %copy.8.weight_ref = bf16[1536,4608]{1,0:T(8,128)(2,1)} copy(bf16[1536,4608]{0,1:T(8,128)(2,1)} %bitcast.1) | data formatting | bytes 28311552 | tf_op jit(solution)/shard_map/reshape | solution.py:460
  51.4 0.0 all-gather.2.cloned.1.call-done.image_ref
  51.4 127.8 %attention_grams.1 = (bf16[256,1536]{1,0:T(8,128)(2,1)}, f32[768,768]{1,0:T(8,128)}, f32[1536,384]{1,0:T(8,128)}) custom-call(bf16[512,1536]{1,0:T(8,128)(2,1)} %all-gather.2.cloned.1.call-done.image_ref, bf16[1536,4608]{1,0:T(8,128)(2,1)} %copy.8.weight_ref), custom_call_target="tpu_custom_call" | custom-call | flops 14000000000 | bytes 24000000 | tf_op jit(solution)/shard_map/attention_grams/pallas_call | solution.py:466
  179.2 2.1 %copy.12 = bf16[256,1536]{1,0:T(8,128)(2,1)} copy(bf16[256,1536]{1,0:T(8,128)(2,1)} %get-tuple-element.12) | data formatting | bytes 1572864
  181.3 0.0 copy-start
  181.3 3.4 %copy.13 = f32[768,768]{1,0:T(8,128)} copy(f32[768,768]{1,0:T(8,128)} %get-tuple-element.13) | data formatting | bytes 4718592
  184.7 0.0 copy-done
  184.7 1.4 copy.14
  (1 shorter events, 0.0 us)
Async XLA Ops:
  7.2 44.2 %all-gather.2.cloned.1.call-start = ((), (), s32[]{:S(2)}) async-start(), calls=%async_computation | async-start | bytes 2359296 | tf_op jit(solution)/shard_map/all_gather | solution.py:458
  181.3 3.4 %copy-start = (f32[1536,384]{1,0:T(8,128)S(1)}, f32[1536,384]{1,0:T(8,128)}, u32[]{:S(2)}) copy-start(f32[1536,384]{1,0:T(8,128)} %get-tuple-element.14) | copy-start | bytes 7077892
Sparse Core Ops, SparseCore 0:
  14.0 27.1 all-gather.1

commit v2 on v1

--- a/solution.py
+++ b/solution.py
@@ -110,13 +110,18 @@
     def valid(self, way, step):
         return self.z >= step if way == 0 else self.z + step < self.length
 
-    def hop(self, way, step):
+    def tokens(self, part):
+        rows = self.rows.shape[1] // 2
+        half = self.x if part == 0 else 1 - self.x
+        return pl.ds(pl.multiple_of(half * rows, rows), rows)
+
+    def hop(self, way, step, part):
         image = self.image(way, step)
         return pltpu.make_async_remote_copy(
-            src_ref=self.rows.at[image],
-            dst_ref=self.rows.at[image],
-            send_sem=self.send.at[way, step],
-            recv_sem=self.receive.at[way, step],
+            src_ref=self.rows.at[image, self.tokens(part)],
+            dst_ref=self.rows.at[image, self.tokens(part)],
+            send_sem=self.send.at[way, step, part],
+            recv_sem=self.receive.at[way, step, part],
             device_id={"dp": self.z + 1 if way == 0 else self.z - 1},
             device_id_type=MESH,
         )
@@ -125,75 +130,97 @@
         inside = self.z < self.length - 1 if way == 0 else self.z > 0
         return inside & self.valid(way, step)
 
-    def arrival(self, way, step):
+    def arrival(self, way, step, part):
         image = self.image(way, step)
         return pltpu.make_async_remote_copy(
-            src_ref=self.rows.at[image],
-            dst_ref=self.rows.at[image],
-            send_sem=self.send.at[way, step],
-            recv_sem=self.receive.at[way, step - 1],
+            src_ref=self.rows.at[image, self.tokens(part)],
+            dst_ref=self.rows.at[image, self.tokens(part)],
+            send_sem=self.send.at[way, step, part],
+            recv_sem=self.receive.at[way, step - 1, part],
             device_id={"dp": self.z - 1 if way == 0 else self.z + 1},
             device_id_type=MESH,
         )
 
-    def sharing(self, source, image, axis):
+    def sharing(self, source, image, axis, part):
         other = {"my": 1 - self.c} if axis == 0 else {"mx": 1 - self.x}
         return pltpu.make_async_remote_copy(
-            src_ref=source.at[image],
-            dst_ref=self.columns.at[image],
-            send_sem=self.share.at[image, axis],
-            recv_sem=self.shared.at[image],
+            src_ref=source.at[image, self.tokens(part)],
+            dst_ref=self.columns.at[image, self.tokens(part)],
+            send_sem=self.share.at[image, axis, self.part_of(part)],
+            recv_sem=self.shared.at[image, self.part_of(part)],
             device_id=other,
             device_id_type=MESH,
         )
 
-    def own(self, image):
+    def part_of(self, part):
+        return self.x if part == 0 else 1 - self.x
+
+    def own(self, image, part):
         return pltpu.make_async_copy(
-            self.rows.at[image], self.columns.at[image], self.local.at[image]
-        )
-
-    def spread(self, image):
+            self.rows.at[image, self.tokens(part)],
+            self.columns.at[image, self.tokens(part)],
+            self.local.at[image, part],
+        )
+
+    def spread(self, image, part):
         @pl.when(self.owner)
         def _():
-            self.sharing(self.rows, image, 1).start()
-            self.sharing(self.rows, image, 0).start()
-            self.own(image).start()
-
-    def begin(self):
+            self.sharing(self.rows, image, 1, part).start()
+            self.sharing(self.rows, image, 0, part).start()
+            self.own(image, part).start()
+
+    def begin(self, part):
         for way in range(2):
 
             @pl.when(self.hops(way, 0))
             def _():
-                self.hop(way, 0).start()
-
-        self.spread(self.z)
-
-    def forward(self, step):
+                self.hop(way, 0, part).start()
+
+        self.spread(self.z, part)
+
+    def forward(self, step, part):
         for way in range(2):
 
             @pl.when(self.valid(way, step))
             def _():
-                self.arrival(way, step).wait_recv()
+                self.arrival(way, step, part).wait_recv()
                 if step < self.length - 1:
 
                     @pl.when(self.hops(way, step))
                     def _():
-                        self.hop(way, step).start()
-
-                self.spread(self.image(way, step))
-
-    def take(self, image, first):
-        @pl.when(self.owner)
-        def _():
-            self.own(image).wait()
+                        self.hop(way, step, part).start()
+
+                self.spread(self.image(way, step), part)
+
+    def follow(self, image, half):
+        rows = self.rows.shape[1] // 2
+        tokens = pl.ds(pl.multiple_of(half * rows, rows), rows)
+        onward = pltpu.make_async_remote_copy(
+            src_ref=self.columns.at[image, tokens],
+            dst_ref=self.columns.at[image, tokens],
+            send_sem=self.share.at[image, 0, half],
+            recv_sem=self.shared.at[image, half],
+            device_id={"my": 1 - self.c},
+            device_id_type=MESH,
+        )
 
         @pl.when(jnp.logical_not(self.owner))
         def _():
-            self.sharing(self.rows, image, 0).wait_recv()
+            onward.wait_recv()
 
         @pl.when(self.relay)
         def _():
-            self.sharing(self.columns, image, 0).start()
+            onward.start()
+
+    def take(self, image, first):
+        for order in range(2):
+
+            @pl.when(self.owner)
+            def _():
+                self.own(image, order).wait()
+
+            half = self.z // 2 if order == 0 else 1 - self.z // 2
+            self.follow(image, half)
 
         def piece(index, carry):
             part = pl.ds(pl.multiple_of(index * 256, 256), 256)
@@ -227,17 +254,20 @@
 
                 @pl.when(self.hops(way, step))
                 def _():
-                    self.hop(way, step).wait_send()
+                    for part in range(2):
+                        self.hop(way, step, part).wait_send()
 
         def one(image, carry):
-            @pl.when(self.owner)
-            def _():
-                self.sharing(self.rows, image, 1).wait_send()
-                self.sharing(self.rows, image, 0).wait_send()
-
-            @pl.when(self.relay)
-            def _():
-                self.sharing(self.columns, image, 0).wait_send()
+            for part in range(2):
+
+                @pl.when(self.owner)
+                def _():
+                    self.sharing(self.rows, image, 1, part).wait_send()
+                    self.sharing(self.rows, image, 0, part).wait_send()
+
+                @pl.when(self.relay)
+                def _():
+                    self.sharing(self.columns, image, 0, part).wait_send()
 
             return carry
 
@@ -246,11 +276,11 @@
 
 def kernel(
     length, factor, head_size,
-    image_ref, weight_ref, context_ref, input_ref, gram_ref,
-    weights, leaving, kept, arrived,
+    normed_ref, weight_ref, context_ref, input_ref, gram_ref,
+    image_ref, weights, leaving, kept, arrived,
     input_rows, input_columns, context_rows, context_columns, total,
     weight_sem, plane_sem, part_send, part_receive,
-    line_send, line_receive, share_send, share_receive, local_sem, swap_sem,
+    line_send, line_receive, share_send, share_receive, local_sem, swap_sem, side_sem,
 ):
     z, x, c = lax.axis_index("dp"), lax.axis_index("mx"), lax.axis_index("my")
     heads, _, triple = weights.shape
@@ -259,9 +289,8 @@
 
     def weight_copy(position):
         head = lax.rem(position + (1 - c) * half, heads)
-        columns = pl.ds(pl.multiple_of(head * triple, triple), triple)
         return pltpu.make_async_copy(
-            weight_ref.at[:, columns], weights.at[position], weight_sem.at[position]
+            weight_ref.at[head], weights.at[position], weight_sem.at[position]
         )
 
     def start_weight(position, carry):
@@ -294,29 +323,56 @@
         line_send.at[1], line_receive.at[1], share_send.at[1], share_receive.at[1], local_sem.at[1],
     )
 
-    def plane_copy():
-        return pltpu.make_async_remote_copy(
-            src_ref=image_ref.at[:, pl.ds(pl.multiple_of((1 - c) * block, block), block)],
-            dst_ref=input_rows.at[z],
-            send_sem=plane_sem.at[0],
-            recv_sem=plane_sem.at[1],
+    side = tokens // 2
+    own_side = pl.ds(pl.multiple_of(x * side, side), side)
+    far_side = pl.ds(pl.multiple_of((1 - x) * side, side), side)
+
+    def side_copy():
+        return pltpu.make_async_remote_copy(
+            src_ref=normed_ref,
+            dst_ref=image_ref.at[own_side],
+            send_sem=side_sem.at[0],
+            recv_sem=side_sem.at[1],
+            device_id={"mx": 1 - x},
+            device_id_type=MESH,
+        )
+
+    def plane_copy(part):
+        away = pl.ds(pl.multiple_of((1 - c) * block, block), block)
+        source = normed_ref.at[:, away] if part == 0 else image_ref.at[far_side, away]
+        return pltpu.make_async_remote_copy(
+            src_ref=source,
+            dst_ref=input_rows.at[z, own_side if part == 0 else far_side],
+            send_sem=plane_sem.at[0, part],
+            recv_sem=plane_sem.at[1, part],
             device_id={"my": 1 - c},
             device_id_type=MESH,
         )
 
-    @pl.when(c == x)
-    def _():
-        plane_copy().start()
+    def start_inputs(part):
         mine = pl.ds(pl.multiple_of(c * block, block), block)
-        keep = pltpu.make_async_copy(image_ref.at[:, mine], input_rows.at[z], plane_sem.at[2])
-        keep.start()
-        keep.wait()
+
+        @pl.when(c == x)
+        def _():
+            if part == 1:
+                side_copy().wait_recv()
+            plane_copy(part).start()
+            if part == 0:
+                input_rows[z, own_side] = normed_ref[:, mine]
+            else:
+                input_rows[z, far_side] = image_ref[far_side, mine]
+
+        @pl.when(c != x)
+        def _():
+            plane_copy(part).wait_recv()
+
+        inputs.begin(part)
 
     @pl.when(c != x)
     def _():
-        plane_copy().wait_recv()
-
-    inputs.begin()
+        side_copy().start()
+
+    start_inputs(0)
 
     def part_copy(index):
         return pltpu.make_async_remote_copy(
@@ -328,26 +384,47 @@
             device_id_type=MESH,
         )
 
-    def project_away(index, carry):
+    def product(rows, position):
+        return jnp.dot(rows, weights[position], preferred_element_type=jnp.float32).astype(
+            jnp.bfloat16
+        )
+
+    def away_near(index, carry):
         weight_copy(index).wait()
-        leaving[index] = jnp.dot(
-            image_ref[...], weights[index], preferred_element_type=jnp.float32
-        ).astype(jnp.bfloat16)
+        leaving[index, own_side] = product(normed_ref[...], index)
+        return carry
+
+    def here_near(index, carry):
+        weight_copy(half + index).wait()
+        kept[index, own_side] = product(normed_ref[...], half + index)
+        return carry
+
+    def away_far(index, carry):
+        leaving[index, far_side] = product(image_ref[far_side], index)
         part_copy(index).start()
         return carry
 
-    lax.fori_loop(0, half, project_away, 0)
-
-    def project_here(index, carry):
-        weight_copy(half + index).wait()
-        kept[index] = jnp.dot(
-            image_ref[...], weights[half + index], preferred_element_type=jnp.float32
-        ).astype(jnp.bfloat16)
+    def here_far(index, carry):
+        kept[index, far_side] = product(image_ref[far_side], half + index)
         return carry
 
-    lax.fori_loop(0, half, project_here, 0)
-
-    inputs.forward(1)
+    lax.fori_loop(0, half, away_near, 0)
+
+    @pl.when(c == x)
+    def _():
+        side_copy().start()
+
+    lax.fori_loop(0, half, here_near, 0)
+    start_inputs(1)
+
+    @pl.when(c != x)
+    def _():
+        side_copy().wait_recv()
+
+    lax.fori_loop(0, half, away_far, 0)
+    inputs.forward(1, 0)
+    lax.fori_loop(0, half, here_far, 0)
+    inputs.forward(1, 1)
 
     def norm(values):
         average = jnp.mean(values, -1, keepdims=True)
@@ -356,12 +433,20 @@
             jnp.bfloat16
         )
 
-    def attend(index, carry):
-        part_copy(index).wait_recv()
-        projected = kept[index].astype(jnp.float32) + arrived[index].astype(jnp.float32)
-        queries = norm(projected[:, :head_size])
-        keys = norm(projected[:, head_size : 2 * head_size])
-        values = projected[:, 2 * head_size :].astype(jnp.bfloat16)
+    def attend(part, index, carry):
+        rows = own_side if part == 0 else far_side
+        if part == 0:
+            part_copy(index).wait_recv()
+
+        def projected(tokens, first, last):
+            return kept[index, tokens, first:last].astype(jnp.float32) + arrived[
+                index, tokens, first:last
+            ].astype(jnp.float32)
+
+        every = slice(None)
+        queries = norm(projected(rows, 0, head_size))
+        keys = norm(projected(every, head_size, 2 * head_size))
+        values = projected(every, 2 * head_size, 3 * head_size).astype(jnp.bfloat16)
         scores = lax.dot_general(
             queries, keys, (((1,), (1,)), ((), ())), preferred_element_type=jnp.float32
         ) * head_size ** (-0.5)
@@ -371,11 +456,14 @@
             powers.astype(jnp.bfloat16), values, preferred_element_type=jnp.float32
         )
         place = pl.ds(pl.multiple_of(index * head_size, head_size), head_size)
-        context_rows[z, :, place] = (mixture / totals).astype(jnp.bfloat16)
+        context_rows[z, rows, place] = (mixture / totals).astype(jnp.bfloat16)
         return carry
 
-    lax.fori_loop(0, half, attend, 0)
-    contexts.begin()
+    lax.fori_loop(0, half, functools.partial(attend, 0), 0)
+    contexts.begin(0)
+    inputs.forward(2, 0)
+    lax.fori_loop(0, half, functools.partial(attend, 1), 0)
+    contexts.begin(1)
 
     own_tokens = tokens // 2
     place = pl.ds(pl.multiple_of(c * block, block), block)
@@ -399,18 +487,22 @@
     context_keep.start()
 
     inputs.consume(0)
-    inputs.forward(2)
+    inputs.forward(2, 1)
     inputs.consume(1)
-    contexts.forward(1)
+    contexts.forward(1, 0)
+    contexts.forward(1, 1)
     contexts.consume(0)
     for step in range(3, length):
-        inputs.forward(step)
+        inputs.forward(step, 0)
+        inputs.forward(step, 1)
         inputs.consume(step - 1)
-        contexts.forward(step - 1)
+        contexts.forward(step - 1, 0)
+        contexts.forward(step - 1, 1)
         contexts.consume(step - 2)
     inputs.consume(length - 1)
     input_ref[...] = input_ref[...] * factor
-    contexts.forward(length - 1)
+    contexts.forward(length - 1, 0)
+    contexts.forward(length - 1, 1)
     contexts.consume(length - 2)
     contexts.consume(length - 1)
 
@@ -433,7 +525,10 @@
 
     @pl.when(c == x)
     def _():
-        plane_copy().wait_send()
+        plane_copy(0).wait_send()
+        plane_copy(1).wait_send()
+
+    side_copy().wait_send()
 
     def part_sent(index, carry):
         part_copy(index).wait_send()
@@ -455,10 +550,10 @@
     average = (row_sums / width)[:, None]
     spread = (row_squares / width)[:, None] - average * average
     normed = ((widened - average) * lax.rsqrt(spread + EPSILON) * ln_gain).astype(jnp.bfloat16)
-    image_rows = lax.all_gather(normed, "mx", axis=0, tiled=True)
     heads, triple = w_qkv.shape[1:]
-    flat_weight = w_qkv.reshape(feature_count, heads * triple)
-    length, tokens, block = lax.axis_size("dp"), image_rows.shape[0], feature_count // 2
+    head_weight = jnp.transpose(w_qkv, (1, 0, 2))
+    tokens = row_count * lax.axis_size("mx")
+    length, block = lax.axis_size("dp"), feature_count // 2
     gathered = pltpu.VMEM((length, tokens, block), jnp.bfloat16)
     part = pltpu.VMEM((heads // 2, tokens, triple), jnp.bfloat16)
     dma = pltpu.SemaphoreType.DMA
@@ -473,20 +568,22 @@
         in_specs=[whole, pl.BlockSpec(memory_space=pl.ANY)],
         out_specs=(whole, whole, whole),
         scratch_shapes=[
+            pltpu.VMEM((tokens, feature_count), jnp.bfloat16),
             pltpu.VMEM((heads, feature_count, triple), jnp.bfloat16),
             part, part, part,
             gathered, gathered, gathered, gathered,
             pltpu.VMEM((block, block), jnp.float32),
             dma((heads,)),
-            dma((3,)),
+            dma((2, 2)),
             dma((heads // 2,)),
             dma((heads // 2,)),
-            dma((2, 2, length)),
-            dma((2, 2, length)),
+            dma((2, 2, length, 2)),
+            dma((2, 2, length, 2)),
+            dma((2, length, 2, 2)),
             dma((2, length, 2)),
-            dma((2, length)),
-            dma((2, length)),
+            dma((2, length, 2)),
             dma((5,)),
+            dma((2,)),
         ],
         compiler_params=pltpu.CompilerParams(
             collective_id=0, has_side_effects=True, vmem_limit_bytes=60 * 1024 * 1024
@@ -495,7 +592,7 @@
             flops=14_000_000_000, bytes_accessed=24_000_000, transcendentals=2_000_000
         ),
         name="attention_grams",
-    )(image_rows, flat_weight)
+    )(normed, head_weight)
 
 
 def solution(mesh):

time: 194 us -> 145 us (0.75)
  local copies, waits for them, and re-layouts: 44.4 us -> 6.84 us
  between operations: 14 us -> 0.64 us
  Pallas kernels: 128 us -> 130 us
    reshape x1 -> x0, local copies, waits for them, and re-layouts: 18.8 us -> none  [on_device_fused(): flat_weight = w_qkv.reshape(feature_count, heads * triple)]
    unnamed x6 -> x5, local copies, waits for them, and re-layouts: 25.6 us -> 6.84 us
    pallas_call x1, Pallas kernels: 128 us -> 130 us  [on_device_fused(): pl.pallas_call(functools.partial(kernel, length, 2.0 / (tokens * length),...]
  transfers between devices with their start and end apart: 1 -> 0, of which waited for: 0 -> 0; matrix products, arithmetic and copies ran while one was open for 19% -> 0% of each run, Pallas kernels for 0% -> 0%
where the time goes in v2:
time: 145 us; the launch traced here: 144 us
  Pallas kernels  130 us (90%)
  local copies, waits for them, and re-layouts  6.84 us (5%)
  other arithmetic  3.82 us (3%)
  blocking collectives  2.8 us (2%)
    pallas_call x1, Pallas kernels, on_device_fused(): pl.pallas_call(functools.partial(kernel, length, 2.0 / (tokens * length),...  130 us
    unnamed x5, local copies, waits for them, and re-layouts  6.84 us

profile of v2, /device:TPU:7, one launch (start us, length us, event | category | flops | bytes accessed | tf_op | source)
XLA Modules:
  0.0 144.4 jit_solution(13265891782776049225)
XLA Ops:
  0.6 1.5 %convert_reduce_fusion = (f32[256]{0:T(256)S(1)}, f32[256]{0:T(256)S(1)}) fusion(bf16[256,1536]{1,0:T(8,128)(2,1)} %param.3), kind=kLoop, calls=%fused_computation.2 | loop fusion | flops 1572352 | bytes 788480 | tf_op jit(solution)/shard_map/reduce_sum | solution.py:548
  2.1 2.8 %all-reduce = (f32[256]{0:T(256)S(1)}, f32[256]{0:T(256)S(1)}) all-reduce(f32[256]{0:T(256)S(1)} %get-tuple-element.4, f32[256]{0:T(256)S(1)} %get-tuple-element.3), channel_id=1, replica_groups=mesh['groups'=2,'dp'=4,'mx'=2,'my'=2] {'my'}, use_global_device_ids=true, to_apply=%region_3.0 | all-reduce | flops 512 | bytes 4096 | tf_op jit(solution)/shard_map/psum | solution.py:548
  4.9 2.3 %fusion.2.normed_ref = bf16[256,1536]{1,0:T(8,128)(2,1)} fusion(bf16[256,1536]{1,0:T(8,128)(2,1)} %param.3, f32[1536]{0:T(1024)} %param.4, f32[256]{0:T(256)S(1)} %get-tuple-element.8, f32[256]{0:T(256)S(1)} %get-tuple-element.7), kind=kLoop, calls=%fused_computation.5 | loop fusion | flops 1966080 | bytes 1581056 | tf_op jit(solution)/shard_map/convert_element_type | solution.py:552
  7.3 130.2 %attention_grams.1 = (bf16[256,1536]{1,0:T(8,128)(2,1)}, f32[768,768]{1,0:T(8,128)}, f32[1536,384]{1,0:T(8,128)}) custom-call(bf16[256,1536]{1,0:T(8,128)(2,1)} %fusion.2.normed_ref, bf16[12,1536,384]{2,1,0:T(8,128)(2,1)} %bitcast.1), custom_call_target="tpu_custom_call" | custom-call | flops 14000000000 | bytes 24000000 | tf_op jit(solution)/shard_map/attention_grams/pallas_call | solution.py:561
  137.5 2.1 %copy.9 = bf16[256,1536]{1,0:T(8,128)(2,1)} copy(bf16[256,1536]{1,0:T(8,128)(2,1)} %get-tuple-element.12) | data formatting | bytes 1572864
  139.6 0.0 copy-start
  139.6 3.4 %copy.10 = f32[768,768]{1,0:T(8,128)} copy(f32[768,768]{1,0:T(8,128)} %get-tuple-element.13) | data formatting | bytes 4718592
  142.9 0.0 copy-done
  142.9 1.4 copy.11
  (1 shorter events, 0.0 us)
Async XLA Ops:
  139.6 3.4 %copy-start = (f32[1536,384]{1,0:T(8,128)S(1)}, f32[1536,384]{1,0:T(8,128)}, u32[]{:S(2)}) copy-start(f32[1536,384]{1,0:T(8,128)} %get-tuple-element.14) | copy-start | bytes 7077892

commit v3 on v2

--- a/solution.py
+++ b/solution.py
@@ -275,12 +275,12 @@
 
 
 def kernel(
-    length, factor, head_size,
-    normed_ref, weight_ref, context_ref, input_ref, gram_ref,
-    image_ref, weights, leaving, kept, arrived,
+    length, head_size,
+    activation_ref, gain_ref, weight_ref, context_ref, input_ref, gram_ref,
+    normed_ref, sums, other_sums, input_total, leaving_gram, image_ref, weights, leaving, kept, arrived,
     input_rows, input_columns, context_rows, context_columns, total,
     weight_sem, plane_sem, part_send, part_receive,
-    line_send, line_receive, share_send, share_receive, local_sem, swap_sem, side_sem,
+    line_send, line_receive, share_send, share_receive, local_sem, swap_sem, side_sem, sum_sem,
 ):
     z, x, c = lax.axis_index("dp"), lax.axis_index("mx"), lax.axis_index("my")
     heads, _, triple = weights.shape
@@ -299,6 +299,22 @@
 
     lax.fori_loop(0, heads, start_weight, 0)
 
+    features = activation_ref.shape[1]
+    tile = 64
+
+    def tile_rows(index):
+        return pl.ds(pl.multiple_of(index * tile, tile), tile)
+
+    def add_up(index, carry):
+        rows = tile_rows(index)
+        values = activation_ref[rows, :].astype(jnp.float32)
+        lanes = (tile, sums.shape[2])
+        sums[0, rows] = jnp.broadcast_to(jnp.sum(values, 1, keepdims=True), lanes)
+        sums[1, rows] = jnp.broadcast_to(jnp.sum(values * values, 1, keepdims=True), lanes)
+        return carry
+
+    lax.fori_loop(0, activation_ref.shape[0] // tile, add_up, 0)
+
     barrier = pltpu.get_barrier_semaphore()
     pl.semaphore_signal(barrier, inc=1, device_id={"my": 1 - c}, device_id_type=MESH)
     pl.semaphore_signal(barrier, inc=1, device_id={"mx": 1 - x}, device_id_type=MESH)
@@ -314,8 +330,33 @@
     edges = jnp.where(z > 0, 1, 0) + jnp.where(z < length - 1, 1, 0)
     pl.semaphore_wait(barrier, 2 + edges)
 
+    def sum_copy():
+        return pltpu.make_async_remote_copy(
+            src_ref=sums,
+            dst_ref=other_sums,
+            send_sem=sum_sem.at[0],
+            recv_sem=sum_sem.at[1],
+            device_id={"my": 1 - c},
+            device_id_type=MESH,
+        )
+
+    sum_copy().start()
+    sum_copy().wait()
+
+    def normalise(index, carry):
+        rows = tile_rows(index)
+        width = features * 2
+        average = (sums[0, rows, 0:1] + other_sums[0, rows, 0:1]) / width
+        squares = (sums[1, rows, 0:1] + other_sums[1, rows, 0:1]) / width
+        values = activation_ref[rows, :].astype(jnp.float32)
+        scale = lax.rsqrt(squares - average * average + EPSILON)
+        normed_ref[rows, :] = ((values - average) * scale * gain_ref[...]).astype(jnp.bfloat16)
+        return carry
+
+    lax.fori_loop(0, activation_ref.shape[0] // tile, normalise, 0)
+
     inputs = Gather(
-        length, (z, x, c), input_rows, input_columns, input_ref,
+        length, (z, x, c), input_rows, input_columns, input_total,
         line_send.at[0], line_receive.at[0], share_send.at[0], share_receive.at[0], local_sem.at[0],
     )
     contexts = Gather(
@@ -500,7 +541,7 @@
         contexts.forward(step - 1, 1)
         contexts.consume(step - 2)
     inputs.consume(length - 1)
-    input_ref[...] = input_ref[...] * factor
+    input_ref[...] = input_total[...].astype(jnp.bfloat16)
     contexts.forward(length - 1, 0)
     contexts.forward(length - 1, 1)
     contexts.consume(length - 2)
@@ -508,11 +549,13 @@
 
     narrow = block // 2
     rows = pl.ds(pl.multiple_of(c * block, block), block)
-    total[...] = total[...] * factor
+    leaving_gram[...] = total[
+        :, pl.ds(pl.multiple_of((1 - c) * narrow, narrow), narrow)
+    ].astype(jnp.bfloat16)
 
     def gram_copy():
         return pltpu.make_async_remote_copy(
-            src_ref=total.at[:, pl.ds(pl.multiple_of((1 - c) * narrow, narrow), narrow)],
+            src_ref=leaving_gram,
             dst_ref=gram_ref.at[rows],
             send_sem=swap_sem.at[3],
             recv_sem=swap_sem.at[4],
@@ -521,7 +564,9 @@
         )
 
     gram_copy().start()
-    gram_ref[rows, :] = total[:, pl.ds(pl.multiple_of(c * narrow, narrow), narrow)]
+    gram_ref[rows, :] = total[
+        :, pl.ds(pl.multiple_of(c * narrow, narrow), narrow)
+    ].astype(jnp.bfloat16)
 
     @pl.when(c == x)
     def _():
@@ -542,14 +587,14 @@
     gram_copy().wait()
 
 
+def widen(factor, context_ref, input_ref, gram_ref, context_out, input_out, gram_out):
+    context_out[...] = context_ref[...]
+    input_out[...] = input_ref[...].astype(jnp.float32) * factor
+    gram_out[...] = gram_ref[...].astype(jnp.float32) * factor
+
+
 def on_device_fused(activations, ln_gain, w_qkv):
     row_count, feature_count = activations.shape
-    widened = activations.astype(jnp.float32)
-    row_sums, row_squares = lax.psum((jnp.sum(widened, 1), jnp.sum(widened * widened, 1)), "my")
-    width = feature_count * lax.axis_size("my")
-    average = (row_sums / width)[:, None]
-    spread = (row_squares / width)[:, None] - average * average
-    normed = ((widened - average) * lax.rsqrt(spread + EPSILON) * ln_gain).astype(jnp.bfloat16)
     heads, triple = w_qkv.shape[1:]
     head_weight = jnp.transpose(w_qkv, (1, 0, 2))
     tokens = row_count * lax.axis_size("mx")
@@ -558,16 +603,18 @@
     part = pltpu.VMEM((heads // 2, tokens, triple), jnp.bfloat16)
     dma = pltpu.SemaphoreType.DMA
     whole = pl.BlockSpec(memory_space=pltpu.VMEM)
-    return pl.pallas_call(
-        functools.partial(kernel, length, 2.0 / (tokens * length), triple // 3),
-        out_shape=(
-            jax.ShapeDtypeStruct((tokens // 2, 2 * block), jnp.bfloat16),
-            jax.ShapeDtypeStruct((block, block), jnp.float32),
-            jax.ShapeDtypeStruct((2 * block, block // 2), jnp.float32),
-        ),
-        in_specs=[whole, pl.BlockSpec(memory_space=pl.ANY)],
+    shapes = ((tokens // 2, 2 * block), (block, block), (2 * block, block // 2))
+    results = pl.pallas_call(
+        functools.partial(kernel, length, triple // 3),
+        out_shape=tuple(jax.ShapeDtypeStruct(shape, jnp.bfloat16) for shape in shapes),
+        in_specs=[whole, whole, pl.BlockSpec(memory_space=pl.ANY)],
         out_specs=(whole, whole, whole),
         scratch_shapes=[
+            pltpu.VMEM((row_count, feature_count), jnp.bfloat16),
+            pltpu.VMEM((2, row_count, 128), jnp.float32),
+            pltpu.VMEM((2, row_count, 128), jnp.float32),
+            pltpu.VMEM((block, block), jnp.float32),
+            pltpu.VMEM((block, block // 2), jnp.bfloat16),
             pltpu.VMEM((tokens, feature_count), jnp.bfloat16),
             pltpu.VMEM((heads, feature_count, triple), jnp.bfloat16),
             part, part, part,
@@ -584,6 +631,7 @@
             dma((2, length, 2)),
             dma((5,)),
             dma((2,)),
+            dma((2,)),
         ],
         compiler_params=pltpu.CompilerParams(
             collective_id=0, has_side_effects=True, vmem_limit_bytes=60 * 1024 * 1024
@@ -592,7 +640,23 @@
             flops=14_000_000_000, bytes_accessed=24_000_000, transcendentals=2_000_000
         ),
         name="attention_grams",
-    )(normed, head_weight)
+    )(activations, ln_gain[None, :], head_weight)
+    steps = 4
+    specs = [pl.BlockSpec((rows // steps, width), lambda i: (i, 0)) for rows, width in shapes]
+    kinds = (jnp.bfloat16, jnp.float32, jnp.float32)
+    return tuple(
+        pl.pallas_call(
+            functools.partial(widen, 2.0 / (tokens * length)),
+            out_shape=tuple(
+                jax.ShapeDtypeStruct(shape, kind) for shape, kind in zip(shapes, kinds)
+            ),
+            grid=(steps,),
+            in_specs=specs,
+            out_specs=tuple(specs),
+            compiler_params=pltpu.CompilerParams(vmem_limit_bytes=60 * 1024 * 1024),
+            name="widen_results",
+        )(*results)
+    )
 
 
 def solution(mesh):

time: 145 us -> 138 us (0.952)
  local copies, waits for them, and re-layouts: 6.84 us -> 1.29 us
  Pallas kernels: 130 us -> 135 us
  other arithmetic: 3.82 us -> 0 us
  blocking collectives: 2.8 us -> 0 us
    unnamed x5 -> x0, local copies, waits for them, and re-layouts: 6.84 us -> none
    pallas_call x1 -> x2, Pallas kernels: 130 us -> 135 us  [the longest x1 131 us: on_device_fused(): pl.pallas_call(functools.partial(kernel, length, triple // 3), out_shape=...]
    psum x1 -> x0, blocking collectives: 2.8 us -> none  [on_device_fused(): lax.psum((jnp.sum(widened, 1), jnp.sum(widened * widened, 1)), 'my')]
    convert_element_type x1 -> x0, other arithmetic: 2.32 us -> none  [on_device_fused(): ((widened - average) * lax.rsqrt(spread + EPSILON) * ln_gain).astype(jnp....]
    reduce_sum x1 -> x0, other arithmetic: 1.48 us -> none  [on_device_fused(): jnp.sum(widened, 1)]
where the time goes in v3:
time: 138 us; the launch traced here: 137 us
  Pallas kernels  135 us (98%)
    pallas_call x1, Pallas kernels, on_device_fused(): pl.pallas_call(functools.partial(kernel, length, triple // 3), out_shape=...  131 us
    pallas_call x1, Pallas kernels, on_device_fused(): pl.pallas_call(functools.partial(widen, 2.0 / (tokens * length)), out_sha...  4.74 us

profile of v3, /device:TPU:7, one launch (start us, length us, event | category | flops | bytes accessed | tf_op | source)
XLA Modules:
  0.0 137.3 jit_solution(17359116426791148442)
XLA Ops:
  0.6 1.3 broadcast_in_dim.3.gain_ref
  1.9 130.7 %attention_grams.1 = (bf16[256,1536]{1,0:T(8,128)(2,1)}, bf16[768,768]{1,0:T(8,128)(2,1)}, bf16[1536,384]{1,0:T(8,128)(2,1)}) custom-call(bf16[256,1536]{1,0:T(8,128)(2,1)} %activation_ref.1, f32[1,1536]{1,0:T(1,128)} %broadcast_in_dim.3.gain_ref, bf16[12,1536,384]{2,1,0:T(8,128)(2,1)} %bitcast.1), custom_call_target="tpu_custom_call" | custom-call | flops 14000000000 | bytes 24000000 | tf_op jit(solution)/shard_map/attention_grams/pallas_call | solution.py:607
  132.6 4.7 %widen_results.1 = (bf16[256,1536]{1,0:T(8,128)(2,1)}, f32[768,768]{1,0:T(8,128)}, f32[1536,384]{1,0:T(8,128)}) custom-call(bf16[256,1536]{1,0:T(8,128)(2,1)} %get-tuple-element.6.context_ref, bf16[768,768]{1,0:T(8,128)(2,1)} %get-tuple-element.7.input_ref, bf16[1536,384]{1,0:T(8,128)(2,1)} %get-tuple-element.8.gram_ref), custom_call_target="tpu_custom_call" | custom-call | tf_op jit(solution)/shard_map/widen_results/pallas_call | solution.py:648

commit v4 on v3

--- a/solution.py
+++ b/solution.py
@@ -350,7 +350,7 @@
         squares = (sums[1, rows, 0:1] + other_sums[1, rows, 0:1]) / width
         values = activation_ref[rows, :].astype(jnp.float32)
         scale = lax.rsqrt(squares - average * average + EPSILON)
-        normed_ref[rows, :] = ((values - average) * scale * gain_ref[...]).astype(jnp.bfloat16)
+        normed_ref[rows, :] = ((values - average) * scale * gain_ref[...][None, :]).astype(jnp.bfloat16)
         return carry
 
     lax.fori_loop(0, activation_ref.shape[0] // tile, normalise, 0)
@@ -542,9 +542,9 @@
         contexts.consume(step - 2)
     inputs.consume(length - 1)
     input_ref[...] = input_total[...].astype(jnp.bfloat16)
+    contexts.consume(length - 2)
     contexts.forward(length - 1, 0)
     contexts.forward(length - 1, 1)
-    contexts.consume(length - 2)
     contexts.consume(length - 1)
 
     narrow = block // 2
@@ -640,7 +640,7 @@
             flops=14_000_000_000, bytes_accessed=24_000_000, transcendentals=2_000_000
         ),
         name="attention_grams",
-    )(activations, ln_gain[None, :], head_weight)
+    )(activations, ln_gain, head_weight)
     steps = 4
     specs = [pl.BlockSpec((rows // steps, width), lambda i: (i, 0)) for rows, width in shapes]
     kinds = (jnp.bfloat16, jnp.float32, jnp.float32)

time: 138 us -> 136 us (0.986)
  no operation moved by 1% of the time
where the time goes in v4:
time: 136 us
  Pallas kernels  135 us (99%)
    pallas_call x1, Pallas kernels, on_device_fused(): pl.pallas_call(functools.partial(kernel, length, triple // 3), out_shape=...  131 us
    pallas_call x1, Pallas kernels, on_device_fused(): pl.pallas_call(functools.partial(widen, 2.0 / (tokens * length)), out_sha...  4.74 us

profile of v4, /device:TPU:7, one launch (start us, length us, event | category | flops | bytes accessed | tf_op | source)
XLA Modules:
  0.0 136.1 jit_solution(3395706663579466035)
XLA Ops:
  0.6 130.7 %attention_grams.1 = (bf16[256,1536]{1,0:T(8,128)(2,1)}, bf16[768,768]{1,0:T(8,128)(2,1)}, bf16[1536,384]{1,0:T(8,128)(2,1)}) custom-call(bf16[256,1536]{1,0:T(8,128)(2,1)} %activation_ref.1, f32[1536]{0:T(1024)} %gain_ref.1, bf16[12,1536,384]{2,1,0:T(8,128)(2,1)} %bitcast.1), custom_call_target="tpu_custom_call" | custom-call | flops 14000000000 | bytes 24000000 | tf_op jit(solution)/shard_map/attention_grams/pallas_call | solution.py:607
  131.3 4.7 %widen_results.1 = (bf16[256,1536]{1,0:T(8,128)(2,1)}, f32[768,768]{1,0:T(8,128)}, f32[1536,384]{1,0:T(8,128)}) custom-call(bf16[256,1536]{1,0:T(8,128)(2,1)} %get-tuple-element.6.context_ref, bf16[768,768]{1,0:T(8,128)(2,1)} %get-tuple-element.7.input_ref, bf16[1536,384]{1,0:T(8,128)(2,1)} %get-tuple-element.8.gram_ref), custom_call_target="tpu_custom_call" | custom-call | tf_op jit(solution)/shard_map/widen_results/pallas_call | solution.py:648
